TPU v7x, 256 devices: a whole 4x4x8 slice. The times are simulated.
256 devices in a mesh: wall: 8 (over x, core), stream: 32 (over z, y).
Axes of the slice: x: 4, y: 4, z: 8, core: 2. Of those that a mesh axis runs over, the one named last changes fastest.
Arguments:
- forcing: float32 [16, 16, 64, 320], P(None, 'wall', 'stream'), may hold values from -72 to 72
- diag_blocks: float32 [16, 64, 320, 320], P('wall', 'stream'), may hold values from -0.04472136 to 2.0447214
- coupling: float32 [4, 16, 64, 320, 320], P(None, 'wall', 'stream'), may hold values from -0.109375 to 0.109375
Outputs:
- solution: float32 [16, 16, 64, 320], P(None, 'wall', 'stream')
- residual: float32 [16, 16, 64, 320], P(None, 'wall', 'stream')
All inputs are finite; a program needn't handle non-finite values.
Results may differ from a plain program's by a relative error of at most 0.0003.
Values sent between devices are 32-bit elements; how exact they have to be, the bound alone decides.
No kernel may reach another device: no remote copies, remote signals or barrier semaphores. Data moves between devices by JAX's collectives and lax.ppermute only.
A program may use at most 64 MiB of HBM per device.

v0:
```python
import jax
import jax.numpy as jnp
from jax import lax
from jax.experimental import pallas as pl
from jax.experimental.pallas import tpu as pltpu
from jax.sharding import PartitionSpec as P

ROWS = 320
BLOCK = 16
STEPS = 4
PANEL = 80
INNER = PANEL - BLOCK
SPAN = 2 * STEPS + 1
basis_shift = 1.5
basis_scale = 0.8

f32 = jnp.float32
bf16 = jnp.bfloat16
highest = lax.Precision.HIGHEST
AXES = ("wall", "stream")
NT = (((1,), (1,)), ((), ()))
VMEM = pl.BlockSpec(memory_space=pltpu.VMEM)
SMEM = pl.BlockSpec(memory_space=pltpu.SMEM)


def groups_by(key):
    found = {}
    for wall in range(8):
        for stream in range(32):
            place = key(wall // 2, wall % 2, stream % 4, stream // 4)
            found.setdefault(place, []).append(wall * 32 + stream)
    return list(found.values())


NEAR = groups_by(lambda x, core, y, z: (y % 2, z))
FAR = groups_by(lambda x, core, y, z: (x, core, y // 2))
COPIES = 16


def call(kernel, name, out_shape, operands, flops, in_specs=None):
    return pl.pallas_call(
        kernel,
        in_specs=in_specs or [VMEM] * len(operands),
        out_specs=jax.tree.map(lambda _: VMEM, out_shape),
        out_shape=out_shape,
        compiler_params=pltpu.CompilerParams(vmem_limit_bytes=16 * 2**20),
        cost_estimate=pl.CostEstimate(flops=flops, bytes_accessed=2**20, transcendentals=0),
        name=name,
    )(*operands)


def shape(*dims, dtype=f32):
    return jax.ShapeDtypeStruct(dims, dtype)


def split(value):
    high = value.astype(bf16)
    return high, (value - high.astype(f32)).astype(bf16)


def prepare_kernel(diag, coupling, local_high, local_low, far_high, far_low):
    element = pl.program_id(0)
    wall, stream = element // 2, element % 2
    row = lax.broadcasted_iota(jnp.int32, (ROWS, ROWS), 0)
    column = lax.broadcasted_iota(jnp.int32, (ROWS, ROWS), 1)

    def store(high, low, at, matrix):
        high_part, low_part = split(matrix * (1.0 / basis_scale))
        high[element, :, at * ROWS : (at + 1) * ROWS] = high_part
        low[element, :, at * ROWS : (at + 1) * ROWS] = low_part

    store(local_high, local_low, 0, diag[0, 0] - jnp.where(row == column, basis_shift, 0.0))
    store(local_high, local_low, 1, coupling[1 - wall, 0, 0])
    store(local_high, local_low, 2, coupling[3 - stream, 0, 0])
    store(far_high, far_low, 0, coupling[wall, 0, 0])
    store(far_high, far_low, 1, coupling[2 + stream, 0, 0])


def prepare(diag_blocks, coupling):
    return pl.pallas_call(
        prepare_kernel,
        grid=(4,),
        in_specs=[
            pl.BlockSpec((1, 1, ROWS, ROWS), lambda e: (e // 2, e % 2, 0, 0)),
            pl.BlockSpec((4, 1, 1, ROWS, ROWS), lambda e: (0, e // 2, e % 2, 0, 0)),
        ],
        out_specs=[VMEM] * 4,
        out_shape=[shape(4, ROWS, 3 * ROWS, dtype=bf16)] * 2
        + [shape(4, ROWS, 2 * ROWS, dtype=bf16)] * 2,
        compiler_params=pltpu.CompilerParams(vmem_limit_bytes=32 * 2**20),
        cost_estimate=pl.CostEstimate(flops=0, bytes_accessed=2**24, transcendentals=0),
        name="prepare",
    )(diag_blocks, coupling)


def times(high, low, sources):
    highs, lows = zip(*[split(source) for source in sources])
    high_source = jnp.concatenate(highs, axis=1)
    both = jnp.concatenate([high_source, jnp.concatenate(lows, axis=1)], axis=0)
    first = lax.dot_general(both, high, NT, preferred_element_type=f32)
    second = lax.dot_general(high_source, low, NT, preferred_element_type=f32)
    return first[:BLOCK] + (first[BLOCK:] + second)


def local_kernel(wall0, wall1, high, low, partial):
    field = (wall0, wall1)
    for w in range(2):
        for s in range(2):
            sources = [field[w][s], field[1 - w][s], field[w][1 - s]]
            partial[w, s] = times(high[2 * w + s], low[2 * w + s], sources)


def far_kernel(inside, partial, below, above, before, behind, high, low, *faces):
    wall_side, stream_side = (below, above), (before, behind)
    for w in range(2):
        for s in range(2):
            sources = [
                jnp.where(inside[w] > 0, wall_side[w][s], 0.0),
                jnp.where(inside[2 + s] > 0, stream_side[s][w], 0.0),
            ]
            value = partial[w, s] + times(high[2 * w + s], low[2 * w + s], sources)
            faces[w][s] = value
            faces[2 + s][w] = value


def start_kernel(forcing, *faces):
    for w in range(2):
        for s in range(2):
            value = forcing[:, w, s, :]
            faces[w][s] = value
            faces[2 + s][w] = value


FACES = [shape(2, BLOCK, ROWS)] * 4


def ring(array, axis, step):
    count = lax.axis_size(axis)
    return lax.ppermute(array, axis, [(i, (i + step) % count) for i in range(count)])


def advance(faces, parts, inside):
    wall0, wall1, stream0, stream1 = faces
    below, above = ring(wall1, "wall", 1), ring(wall0, "wall", -1)
    before, behind = ring(stream1, "stream", 1), ring(stream0, "stream", -1)
    local_high, local_low, far_high, far_low = parts
    partial = call(
        local_kernel, "local", shape(2, 2, BLOCK, ROWS), (wall0, wall1, local_high, local_low), 10**9
    )
    return call(
        far_kernel,
        "far",
        FACES,
        (inside, partial, below, above, before, behind, far_high, far_low),
        10**9,
        in_specs=[SMEM] + [VMEM] * 7,
    )


def pack_gram(panels):
    gram = sum(
        lax.dot_general(p, p, NT, precision=highest, preferred_element_type=f32) for p in panels
    )
    first = jnp.concatenate([gram[:16], gram[48:64, 48:], gram[64:, 64:]], axis=1)
    second = jnp.concatenate([gram[16:32, 16:], gram[32:48, 32:], jnp.zeros((16, 16), f32)], axis=1)
    return jnp.concatenate([first, second], axis=0)


def unpack_gram(packed):
    first, second = packed[:16], packed[16:]
    zeros = lambda width: jnp.zeros((16, width), f32)
    upper = jnp.concatenate(
        [
            jnp.concatenate([first[:, :80], zeros(48)], axis=1),
            jnp.concatenate([zeros(16), second[:, :64], zeros(48)], axis=1),
            jnp.concatenate([zeros(32), second[:, 64:112], zeros(48)], axis=1),
            jnp.concatenate([zeros(48), first[:, 80:112], zeros(48)], axis=1),
            jnp.concatenate([zeros(64), first[:, 112:], zeros(48)], axis=1),
            jnp.zeros((48, 128), f32),
        ],
        axis=0,
    )
    row = lax.broadcasted_iota(jnp.int32, (128, 128), 0) // BLOCK
    column = lax.broadcasted_iota(jnp.int32, (128, 128), 1) // BLOCK
    return jnp.where(row <= column, upper, upper.T)


def small_solve(gram):
    right = basis_shift * gram[:PANEL, :INNER] + basis_scale * gram[:PANEL, BLOCK:PANEL]
    normal = basis_shift * right[:INNER] + basis_scale * right[BLOCK:]
    target = basis_shift * gram[:INNER, :BLOCK] + basis_scale * gram[BLOCK:PANEL, :BLOCK]
    system = jnp.concatenate([normal, target, jnp.zeros((INNER, 48), f32)], axis=1)
    rows = lax.broadcasted_iota(jnp.int32, (INNER, 128), 0)
    group = 4
    for start in range(0, INNER, group):
        columns = [
            jnp.broadcast_to(system[:, start + j : start + j + 1], (INNER, 128))
            for j in range(group)
        ]
        for j in range(group):
            k = start + j
            inverse = 1.0 / columns[j][k : k + 1]
            pivot_row = system[k : k + 1] * inverse
            system = jnp.where(rows == k, pivot_row, system - columns[j] * pivot_row)
            for later in range(j + 1, group):
                scaled = columns[later][k : k + 1] * inverse
                columns[later] = jnp.where(
                    rows == k, scaled, columns[later] - columns[j] * scaled
                )
    coefficients = system[:, INNER:PANEL]
    zero = jnp.zeros((BLOCK, BLOCK), f32)
    update = basis_shift * jnp.concatenate([coefficients, zero], axis=0)
    update = update + basis_scale * jnp.concatenate([zero, coefficients], axis=0)
    return coefficients, update


def transposed(value):
    return value.T


def spread(packed, copies):
    copies[...] = jnp.broadcast_to(packed[None], copies.shape)


def element_panels(powers):
    count = len(powers) // 2
    return [
        jnp.concatenate([powers[2 * j + w][s] for j in range(count)], axis=0)
        for w in range(2)
        for s in range(2)
    ]


def gram_kernel(*refs):
    spread(pack_gram(element_panels(refs[:-1])), refs[-1])


def resum_kernel(received, copies):
    spread(jnp.sum(received[...], axis=0), copies)


def device_sum(copies):
    received = lax.all_to_all(copies, AXES, 0, 0, axis_index_groups=NEAR)
    copies = call(resum_kernel, "resum", shape(COPIES, 32, 128), (received,), 10**6)
    return lax.all_to_all(copies, AXES, 0, 0, axis_index_groups=FAR)


def restart_kernel(received, *refs):
    powers, (solution, basis, copies) = refs[:-3], refs[-3:]
    coefficients, update = small_solve(unpack_gram(jnp.sum(received[...], axis=0)))
    update = -transposed(update)
    width = SPAN * BLOCK
    lines = [
        jnp.concatenate(
            [
                jnp.zeros((BLOCK, BLOCK * j), f32),
                update,
                jnp.zeros((BLOCK, width - PANEL - BLOCK * j), f32),
            ][(0 if j else 1) : (3 if j < STEPS else 2)],
            axis=1,
        )
        for j in range(STEPS + 1)
    ]
    lines.append(
        jnp.concatenate([transposed(coefficients), jnp.zeros((BLOCK, width - INNER), f32)], axis=1)
    )
    weights = jnp.concatenate(lines, axis=0)
    panels = []
    for e, panel in enumerate(element_panels(powers)):
        mixed = jnp.dot(weights, panel, precision=highest, preferred_element_type=f32)
        panels.append(panel[:PANEL] + mixed[:PANEL])
        basis[e] = panels[-1]
        solution[e] = mixed[PANEL:]
    spread(pack_gram(panels), copies)


def finish_kernel(received, solution, basis, solution_out, residual_out):
    coefficients, update = small_solve(unpack_gram(jnp.sum(received[...], axis=0)))
    weights = jnp.concatenate(
        [
            jnp.concatenate([transposed(coefficients), jnp.zeros((BLOCK, BLOCK), f32)], axis=1),
            -transposed(update),
        ],
        axis=0,
    )
    for w in range(2):
        for s in range(2):
            e = 2 * w + s
            panel = basis[e]
            mixed = jnp.dot(weights, panel, precision=highest, preferred_element_type=f32)
            solution_out[:, w, s, :] = solution[e] + mixed[:BLOCK]
            residual_out[:, w, s, :] = panel[:BLOCK] + mixed[BLOCK:]


def on_device(forcing, diag_blocks, coupling):
    wall, stream = lax.axis_index("wall"), lax.axis_index("stream")
    inside = jnp.stack([wall > 0, wall < 7, stream > 0, stream < 31]).astype(jnp.int32)
    faces = call(start_kernel, "start", FACES, (forcing,), 10**6)
    parts = prepare(diag_blocks, coupling)
    powers = [*faces[:2]]
    received = None
    for step in range(2 * STEPS):
        faces = advance(faces, parts, inside)
        powers += faces[:2]
        if step == STEPS - 1:
            copies = call(gram_kernel, "gram", shape(COPIES, 32, 128), powers, 10**7)
            received = device_sum(copies)
    solution, basis, copies = call(
        restart_kernel,
        "restart",
        [shape(4, BLOCK, ROWS), shape(4, PANEL, ROWS), shape(COPIES, 32, 128)],
        (received, *powers),
        10**8,
    )
    return call(
        finish_kernel,
        "finish",
        [shape(BLOCK, 2, 2, ROWS)] * 2,
        (device_sum(copies), solution, basis),
        10**8,
    )


def solution(mesh):
    return jax.shard_map(
        on_device,
        mesh=mesh,
        in_specs=(
            P(None, "wall", "stream", None),
            P("wall", "stream", None, None),
            P(None, "wall", "stream", None, None),
        ),
        out_specs=(P(None, "wall", "stream", None), P(None, "wall", "stream", None)),
        check_vma=False,
    )
```

profile of v0, /device:TPU:1, one launch (start us, length us, event | category | flops | bytes accessed | tf_op | source)
XLA Modules:
  0.0 166.5 jit_solution(5042844639578298847)
XLA Ops:
  1.6 2.2 %collective-permute-start.2 = (f32[2,16,320]{2,1,0:T(8,128)S(1)}, f32[2,16,320]{2,1,0:T(8,128)S(1)}, u32[]{:S(2)}, u32[]{:S(2)}) collective-permute-start(f32[2,16,320]{2,1,0:T(8,128)S(1)} %get-tuple-element.47), channel_id=1, source_target_pairs={{0,1},{1,2},{2,3},{3,4},{4,5},{5,6},{6,7},{7,8},{8,9},{9,10},{10,1... | collective-permute-start | bytes 122888 | tf_op jit(solution)/shard_map/ppermute | solution.py:139
  3.8 6.8 %collective-permute-start.3 = (f32[2,16,320]{2,1,0:T(8,128)S(1)}, f32[2,16,320]{2,1,0:T(8,128)S(1)}, u32[]{:S(2)}, u32[]{:S(2)}) collective-permute-start(f32[2,16,320]{2,1,0:T(8,128)S(1)} %get-tuple-element.48), channel_id=1, source_target_pairs={{0,31},{1,0},{2,1},{3,2},{4,3},{5,4},{6,5},{7,6},{8,7},{9,8},{10,9... | collective-permute-start | bytes 122888 | tf_op jit(solution)/shard_map/ppermute | solution.py:139
  12.6 3.2 %copy-done.4 = f32[4,2,2,320,320]{4,3,2,1,0:T(8,128)S(1)} copy-done((f32[4,2,2,320,320]{4,3,2,1,0:T(8,128)S(1)}, f32[4,2,2,320,320]{4,3,2,1,0:T(8,128)}, u32[]{:S(2)}) %copy-start.4) | copy-done | bytes 6553624
  17.4 4.0 %prepare.1 = (bf16[4,320,960]{2,1,0:T(8,128)(2,1)S(1)}, bf16[4,320,960]{2,1,0:T(8,128)(2,1)S(1)}, bf16[4,320,640]{2,1,0:T(8,128)(2,1)S(1)}, bf16[4,320,640]{2,1,0:T(8,128)(2,1)S(1)}) custom-call(f32[2,2,320,320]{3,2,1,0:T(8,128)S(1)} %copy-done.5, f32[4,2,2,320,320]{4,3,2,1,0:T(8,128)S(1)} %copy-done.4), custom_call_target="tpu_custom_call" | custom-call | bytes 16777216 | tf_op jit(solution)/shard_map/prepare/pallas_call | solution.py:80
  24.7 4.8 %collective-permute-start.7 = (f32[2,16,320]{2,1,0:T(8,128)S(1)}, f32[2,16,320]{2,1,0:T(8,128)S(1)}, u32[]{:S(2)}, u32[]{:S(2)}) collective-permute-start(f32[2,16,320]{2,1,0:T(8,128)S(1)} %get-tuple-element.54), channel_id=1, source_target_pairs={{0,31},{1,0},{2,1},{3,2},{4,3},{5,4},{6,5},{7,6},{8,7},{9,8},{10,9... | collective-permute-start | bytes 122888 | tf_op jit(solution)/shard_map/ppermute | solution.py:139
  35.5 4.8 %collective-permute-start.11 = (f32[2,16,320]{2,1,0:T(8,128)S(1)}, f32[2,16,320]{2,1,0:T(8,128)S(1)}, u32[]{:S(2)}, u32[]{:S(2)}) collective-permute-start(f32[2,16,320]{2,1,0:T(8,128)S(1)} %get-tuple-element.58), channel_id=1, source_target_pairs={{0,31},{1,0},{2,1},{3,2},{4,3},{5,4},{6,5},{7,6},{8,7},{9,8},{10,9... | collective-permute-start | bytes 122888 | tf_op jit(solution)/shard_map/ppermute | solution.py:139
  40.3 4.6 %collective-permute-start.9 = (f32[2,16,320]{2,1,0:T(8,128)S(1)}, f32[2,16,320]{2,1,0:T(8,128)S(1)}, u32[]{:S(2)}, u32[]{:S(2)}) collective-permute-start(f32[2,16,320]{2,1,0:T(8,128)S(1)} %get-tuple-element.55.wall0.refs_4_), channel_id=1, source_target_pairs={{0,224},{32,0},{64,32},{96,64},{128,96},{160,128},{192,160},{224,1... | collective-permute-start | bytes 122888 | tf_op jit(solution)/shard_map/ppermute | solution.py:139
  48.0 4.8 %collective-permute-start.15 = (f32[2,16,320]{2,1,0:T(8,128)S(1)}, f32[2,16,320]{2,1,0:T(8,128)S(1)}, u32[]{:S(2)}, u32[]{:S(2)}) collective-permute-start(f32[2,16,320]{2,1,0:T(8,128)S(1)} %get-tuple-element.62), channel_id=1, source_target_pairs={{0,31},{1,0},{2,1},{3,2},{4,3},{5,4},{6,5},{7,6},{8,7},{9,8},{10,9... | collective-permute-start | bytes 122888 | tf_op jit(solution)/shard_map/ppermute | solution.py:139
  52.8 3.7 %collective-permute-start.13 = (f32[2,16,320]{2,1,0:T(8,128)S(1)}, f32[2,16,320]{2,1,0:T(8,128)S(1)}, u32[]{:S(2)}, u32[]{:S(2)}) collective-permute-start(f32[2,16,320]{2,1,0:T(8,128)S(1)} %get-tuple-element.59.wall0.refs_6_), channel_id=1, source_target_pairs={{0,224},{32,0},{64,32},{96,64},{128,96},{160,128},{192,160},{224,1... | collective-permute-start | bytes 122888 | tf_op jit(solution)/shard_map/ppermute | solution.py:139
  61.8 6.5 %all-to-all-start = ((f32[16,32,128]{2,1,0:T(8,128)}), f32[16,32,128]{2,1,0:T(8,128)S(1)}, u32[]{:S(2)}, u32[]{:S(2)}) async-start(f32[16,32,128]{2,1,0:T(8,128)} %gram.1), calls=%async_computation | async-start | bytes 524288 | tf_op jit(solution)/shard_map/all_to_all | solution.py:243
  70.0 4.8 %collective-permute-start.19 = (f32[2,16,320]{2,1,0:T(8,128)S(1)}, f32[2,16,320]{2,1,0:T(8,128)S(1)}, u32[]{:S(2)}, u32[]{:S(2)}) collective-permute-start(f32[2,16,320]{2,1,0:T(8,128)S(1)} %get-tuple-element.66), channel_id=1, source_target_pairs={{0,31},{1,0},{2,1},{3,2},{4,3},{5,4},{6,5},{7,6},{8,7},{9,8},{10,9... | collective-permute-start | bytes 122888 | tf_op jit(solution)/shard_map/ppermute | solution.py:139
  78.5 2.2 %far.12 = (f32[2,16,320]{2,1,0:T(8,128)S(1)}, f32[2,16,320]{2,1,0:T(8,128)S(1)}, f32[2,16,320]{2,1,0:T(8,128)}, f32[2,16,320]{2,1,0:T(8,128)}) custom-call(s32[4]{0:T(128)S(1)} %add_convert_fusion.inside, f32[2,2,16,320]{3,2,1,0:T(8,128)S(1)} %local.12.partial, f32[2,16,320]{2,1,0:T(8,128)S(1)} %collective-permute-done.16.below, ...), custom_call_target="tpu_custom_call" | custom-call | flops 1000000000 | bytes 1048576 | tf_op jit(solution)/shard_map/far/pallas_call | solution.py:41
  80.7 4.8 %collective-permute-start.23 = (f32[2,16,320]{2,1,0:T(8,128)}, f32[2,16,320]{2,1,0:T(8,128)}, u32[]{:S(2)}, u32[]{:S(2)}) collective-permute-start(f32[2,16,320]{2,1,0:T(8,128)} %get-tuple-element.70), channel_id=1, source_target_pairs={{0,31},{1,0},{2,1},{3,2},{4,3},{5,4},{6,5},{7,6},{8,7},{9,8},{10,9... | collective-permute-start | bytes 122888 | tf_op jit(solution)/shard_map/ppermute | solution.py:139
  85.5 2.4 %collective-permute-start.21 = (f32[2,16,320]{2,1,0:T(8,128)S(1)}, f32[2,16,320]{2,1,0:T(8,128)}, u32[]{:S(2)}, u32[]{:S(2)}) collective-permute-start(f32[2,16,320]{2,1,0:T(8,128)S(1)} %get-tuple-element.67.wall0.refs_10_), channel_id=1, source_target_pairs={{0,224},{32,0},{64,32},{96,64},{128,96},{160,128},{192,160},{224,1... | collective-permute-start | bytes 122888 | tf_op jit(solution)/shard_map/ppermute | solution.py:139
  88.7 5.0 %all-to-all-start.1 = ((f32[16,32,128]{2,1,0:T(8,128)}), f32[16,32,128]{2,1,0:T(8,128)S(1)}, u32[]{:S(2)}, u32[]{:S(2)}) async-start(f32[16,32,128]{2,1,0:T(8,128)} %resum.2), calls=%async_computation.1 | async-start | bytes 524288 | tf_op jit(solution)/shard_map/all_to_all | solution.py:245
  101.8 3.4 %collective-permute-start.27 = (f32[2,16,320]{2,1,0:T(8,128)S(1)}, f32[2,16,320]{2,1,0:T(8,128)S(1)}, u32[]{:S(2)}, u32[]{:S(2)}) collective-permute-start(f32[2,16,320]{2,1,0:T(8,128)S(1)} %get-tuple-element.74), channel_id=1, source_target_pairs={{0,31},{1,0},{2,1},{3,2},{4,3},{5,4},{6,5},{7,6},{8,7},{9,8},{10,9... | collective-permute-start | bytes 122888 | tf_op jit(solution)/shard_map/ppermute | solution.py:139
  105.3 2.7 %collective-permute-start.25 = (f32[2,16,320]{2,1,0:T(8,128)S(1)}, f32[2,16,320]{2,1,0:T(8,128)S(1)}, u32[]{:S(2)}, u32[]{:S(2)}) collective-permute-start(f32[2,16,320]{2,1,0:T(8,128)S(1)} %get-tuple-element.71.wall0.refs_12_), channel_id=1, source_target_pairs={{0,224},{32,0},{64,32},{96,64},{128,96},{160,128},{192,160},{224,1... | collective-permute-start | bytes 122888 | tf_op jit(solution)/shard_map/ppermute | solution.py:139
  112.7 4.8 %collective-permute-start.31 = (f32[2,16,320]{2,1,0:T(8,128)S(1)}, f32[2,16,320]{2,1,0:T(8,128)S(1)}, u32[]{:S(2)}, u32[]{:S(2)}) collective-permute-start(f32[2,16,320]{2,1,0:T(8,128)S(1)} %get-tuple-element.78), channel_id=1, source_target_pairs={{0,31},{1,0},{2,1},{3,2},{4,3},{5,4},{6,5},{7,6},{8,7},{9,8},{10,9... | collective-permute-start | bytes 122888 | tf_op jit(solution)/shard_map/ppermute | solution.py:139
  117.4 4.6 %collective-permute-start.29 = (f32[2,16,320]{2,1,0:T(8,128)S(1)}, f32[2,16,320]{2,1,0:T(8,128)S(1)}, u32[]{:S(2)}, u32[]{:S(2)}) collective-permute-start(f32[2,16,320]{2,1,0:T(8,128)S(1)} %get-tuple-element.75.wall0.refs_14_), channel_id=1, source_target_pairs={{0,224},{32,0},{64,32},{96,64},{128,96},{160,128},{192,160},{224,1... | collective-permute-start | bytes 122888 | tf_op jit(solution)/shard_map/ppermute | solution.py:139
  123.6 2.2 %far.15 = (f32[2,16,320]{2,1,0:T(8,128)S(1)}, f32[2,16,320]{2,1,0:T(8,128)S(1)}, f32[2,16,320]{2,1,0:T(8,128)}, f32[2,16,320]{2,1,0:T(8,128)}) custom-call(s32[4]{0:T(128)S(1)} %add_convert_fusion.inside, f32[2,2,16,320]{3,2,1,0:T(8,128)S(1)} %local.15.partial, f32[2,16,320]{2,1,0:T(8,128)S(1)} %collective-permute-done.28.below, ...), custom_call_target="tpu_custom_call" | custom-call | flops 1000000000 | bytes 1048576 | tf_op jit(solution)/shard_map/far/pallas_call | solution.py:41
  125.8 4.3 %restart.1 = (f32[4,16,320]{2,1,0:T(8,128)S(1)}, f32[4,80,320]{2,1,0:T(8,128)S(1)}, f32[16,32,128]{2,1,0:T(8,128)S(1)}) custom-call(f32[16,32,128]{2,1,0:T(8,128)S(1)} %all-to-all-done.1.received, f32[2,16,320]{2,1,0:T(8,128)S(1)} %get-tuple-element.43.wall0.refs_0_, f32[2,16,320]{2,1,0:T(8,128)S(1)} %get-tuple-element.44.wall1.refs_1_, ...), custom_call_target="tpu_custom_call" | custom-call | flops 100000000 | bytes 1048576 | tf_op jit(solution)/shard_map/restart/pallas_call | solution.py:41
  130.1 15.0 %all_to_all.20.received = f32[16,32,128]{2,1,0:T(8,128)S(1)} all-to-all(f32[16,32,128]{2,1,0:T(8,128)S(1)} %get-tuple-element.81), channel_id=1, replica_groups={{0,2,32,34,64,66,96,98,128,130,160,162,192,194,224,226},{1,3,33,35,65,6..., dimensions={0} | all-to-all | bytes 524288 | tf_op jit(solution)/shard_map/all_to_all | solution.py:243
  145.2 17.4 %all_to_all.21.received = f32[16,32,128]{2,1,0:T(8,128)S(1)} all-to-all(f32[16,32,128]{2,1,0:T(8,128)S(1)} %resum.3), channel_id=1, replica_groups={{0,1,4,5,8,9,12,13,16,17,20,21,24,25,28,29},{2,3,6,7,10,11,14,15,18,19,..., dimensions={0} | all-to-all | bytes 524288 | tf_op jit(solution)/shard_map/all_to_all | solution.py:245
  162.6 3.9 %finish.1 = (f32[16,2,2,320]{3,2,1,0:T(2,128)}, f32[16,2,2,320]{3,2,1,0:T(2,128)}) custom-call(f32[16,32,128]{2,1,0:T(8,128)S(1)} %all_to_all.21.received, f32[4,16,320]{2,1,0:T(8,128)S(1)} %get-tuple-element.82.solution, f32[4,80,320]{2,1,0:T(8,128)S(1)} %get-tuple-element.83.basis), custom_call_target="tpu_custom_call" | custom-call | flops 100000000 | bytes 1048576 | tf_op jit(solution)/shard_map/finish/pallas_call | solution.py:41
  (114 shorter events, 42.7 us)
Async XLA Ops:
  1.6 21.4 %collective-permute-start.2 = (f32[2,16,320]{2,1,0:T(8,128)S(1)}, f32[2,16,320]{2,1,0:T(8,128)S(1)}, u32[]{:S(2)}, u32[]{:S(2)}) collective-permute-start(f32[2,16,320]{2,1,0:T(8,128)S(1)} %get-tuple-element.47), channel_id=1, source_target_pairs={{0,1},{1,2},{2,3},{3,4},{4,5},{5,6},{6,7},{7,8},{8,9},{9,10},{10,1... | collective-permute-start | bytes 122888 | tf_op jit(solution)/shard_map/ppermute | solution.py:139
  3.8 19.2 %collective-permute-start.3 = (f32[2,16,320]{2,1,0:T(8,128)S(1)}, f32[2,16,320]{2,1,0:T(8,128)S(1)}, u32[]{:S(2)}, u32[]{:S(2)}) collective-permute-start(f32[2,16,320]{2,1,0:T(8,128)S(1)} %get-tuple-element.48), channel_id=1, source_target_pairs={{0,31},{1,0},{2,1},{3,2},{4,3},{5,4},{6,5},{7,6},{8,7},{9,8},{10,9... | collective-permute-start | bytes 122888 | tf_op jit(solution)/shard_map/ppermute | solution.py:139
  10.6 12.5 %collective-permute-start.1 = (f32[2,16,320]{2,1,0:T(8,128)S(1)}, f32[2,16,320]{2,1,0:T(8,128)S(1)}, u32[]{:S(2)}, u32[]{:S(2)}) collective-permute-start(f32[2,16,320]{2,1,0:T(8,128)S(1)} %get-tuple-element.43.wall0.refs_0_), channel_id=1, source_target_pairs={{0,224},{32,0},{64,32},{96,64},{128,96},{160,128},{192,160},{224,1... | collective-permute-start | bytes 122888 | tf_op jit(solution)/shard_map/ppermute | solution.py:139
  11.5 11.5 %collective-permute-start = (f32[2,16,320]{2,1,0:T(8,128)S(1)}, f32[2,16,320]{2,1,0:T(8,128)S(1)}, u32[]{:S(2)}, u32[]{:S(2)}) collective-permute-start(f32[2,16,320]{2,1,0:T(8,128)S(1)} %get-tuple-element.44.wall1.refs_1_), channel_id=1, source_target_pairs={{0,32},{32,64},{64,96},{96,128},{128,160},{160,192},{192,224},{224... | collective-permute-start | bytes 122888 | tf_op jit(solution)/shard_map/ppermute | solution.py:139
  24.6 8.0 %collective-permute-start.6 = (f32[2,16,320]{2,1,0:T(8,128)S(1)}, f32[2,16,320]{2,1,0:T(8,128)S(1)}, u32[]{:S(2)}, u32[]{:S(2)}) collective-permute-start(f32[2,16,320]{2,1,0:T(8,128)S(1)} %get-tuple-element.53), channel_id=1, source_target_pairs={{0,1},{1,2},{2,3},{3,4},{4,5},{5,6},{6,7},{7,8},{8,9},{9,10},{10,1... | collective-permute-start | bytes 122888 | tf_op jit(solution)/shard_map/ppermute | solution.py:139
  24.7 8.0 %collective-permute-start.7 = (f32[2,16,320]{2,1,0:T(8,128)S(1)}, f32[2,16,320]{2,1,0:T(8,128)S(1)}, u32[]{:S(2)}, u32[]{:S(2)}) collective-permute-start(f32[2,16,320]{2,1,0:T(8,128)S(1)} %get-tuple-element.54), channel_id=1, source_target_pairs={{0,31},{1,0},{2,1},{3,2},{4,3},{5,4},{6,5},{7,6},{8,7},{9,8},{10,9... | collective-permute-start | bytes 122888 | tf_op jit(solution)/shard_map/ppermute | solution.py:139
  35.5 10.9 %collective-permute-start.10 = (f32[2,16,320]{2,1,0:T(8,128)S(1)}, f32[2,16,320]{2,1,0:T(8,128)S(1)}, u32[]{:S(2)}, u32[]{:S(2)}) collective-permute-start(f32[2,16,320]{2,1,0:T(8,128)S(1)} %get-tuple-element.57), channel_id=1, source_target_pairs={{0,1},{1,2},{2,3},{3,4},{4,5},{5,6},{6,7},{7,8},{8,9},{9,10},{10,1... | collective-permute-start | bytes 122888 | tf_op jit(solution)/shard_map/ppermute | solution.py:139
  35.5 10.8 %collective-permute-start.11 = (f32[2,16,320]{2,1,0:T(8,128)S(1)}, f32[2,16,320]{2,1,0:T(8,128)S(1)}, u32[]{:S(2)}, u32[]{:S(2)}) collective-permute-start(f32[2,16,320]{2,1,0:T(8,128)S(1)} %get-tuple-element.58), channel_id=1, source_target_pairs={{0,31},{1,0},{2,1},{3,2},{4,3},{5,4},{6,5},{7,6},{8,7},{9,8},{10,9... | collective-permute-start | bytes 122888 | tf_op jit(solution)/shard_map/ppermute | solution.py:139
  48.0 10.0 %collective-permute-start.14 = (f32[2,16,320]{2,1,0:T(8,128)S(1)}, f32[2,16,320]{2,1,0:T(8,128)S(1)}, u32[]{:S(2)}, u32[]{:S(2)}) collective-permute-start(f32[2,16,320]{2,1,0:T(8,128)S(1)} %get-tuple-element.61), channel_id=1, source_target_pairs={{0,1},{1,2},{2,3},{3,4},{4,5},{5,6},{6,7},{7,8},{8,9},{9,10},{10,1... | collective-permute-start | bytes 122888 | tf_op jit(solution)/shard_map/ppermute | solution.py:139
  48.0 10.0 %collective-permute-start.15 = (f32[2,16,320]{2,1,0:T(8,128)S(1)}, f32[2,16,320]{2,1,0:T(8,128)S(1)}, u32[]{:S(2)}, u32[]{:S(2)}) collective-permute-start(f32[2,16,320]{2,1,0:T(8,128)S(1)} %get-tuple-element.62), channel_id=1, source_target_pairs={{0,31},{1,0},{2,1},{3,2},{4,3},{5,4},{6,5},{7,6},{8,7},{9,8},{10,9... | collective-permute-start | bytes 122888 | tf_op jit(solution)/shard_map/ppermute | solution.py:139
  61.8 26.1 %all-to-all-start = ((f32[16,32,128]{2,1,0:T(8,128)}), f32[16,32,128]{2,1,0:T(8,128)S(1)}, u32[]{:S(2)}, u32[]{:S(2)}) async-start(f32[16,32,128]{2,1,0:T(8,128)} %gram.1), calls=%async_computation | async-start | bytes 524288 | tf_op jit(solution)/shard_map/all_to_all | solution.py:243
  68.3 9.8 %collective-permute-start.17 = (f32[2,16,320]{2,1,0:T(8,128)S(1)}, f32[2,16,320]{2,1,0:T(8,128)S(1)}, u32[]{:S(2)}, u32[]{:S(2)}) collective-permute-start(f32[2,16,320]{2,1,0:T(8,128)S(1)} %get-tuple-element.63.refs_8_.wall0), channel_id=1, source_target_pairs={{0,224},{32,0},{64,32},{96,64},{128,96},{160,128},{192,160},{224,1... | collective-permute-start | bytes 122888 | tf_op jit(solution)/shard_map/ppermute | solution.py:139
  68.5 9.6 %collective-permute-start.16 = (f32[2,16,320]{2,1,0:T(8,128)S(1)}, f32[2,16,320]{2,1,0:T(8,128)S(1)}, u32[]{:S(2)}, u32[]{:S(2)}) collective-permute-start(f32[2,16,320]{2,1,0:T(8,128)S(1)} %get-tuple-element.64.refs_9_.wall1), channel_id=1, source_target_pairs={{0,32},{32,64},{64,96},{96,128},{128,160},{160,192},{192,224},{224... | collective-permute-start | bytes 122888 | tf_op jit(solution)/shard_map/ppermute | solution.py:139
  70.0 8.0 %collective-permute-start.18 = (f32[2,16,320]{2,1,0:T(8,128)}, f32[2,16,320]{2,1,0:T(8,128)S(1)}, u32[]{:S(2)}, u32[]{:S(2)}) collective-permute-start(f32[2,16,320]{2,1,0:T(8,128)} %copy-done.21), channel_id=1, source_target_pairs={{0,1},{1,2},{2,3},{3,4},{4,5},{5,6},{6,7},{7,8},{8,9},{9,10},{10,1... | collective-permute-start | bytes 122888 | tf_op jit(solution)/shard_map/ppermute | solution.py:139
  70.0 8.0 %collective-permute-start.19 = (f32[2,16,320]{2,1,0:T(8,128)S(1)}, f32[2,16,320]{2,1,0:T(8,128)S(1)}, u32[]{:S(2)}, u32[]{:S(2)}) collective-permute-start(f32[2,16,320]{2,1,0:T(8,128)S(1)} %get-tuple-element.66), channel_id=1, source_target_pairs={{0,31},{1,0},{2,1},{3,2},{4,3},{5,4},{6,5},{7,6},{8,7},{9,8},{10,9... | collective-permute-start | bytes 122888 | tf_op jit(solution)/shard_map/ppermute | solution.py:139
  80.7 16.2 %collective-permute-start.22 = (f32[2,16,320]{2,1,0:T(8,128)}, f32[2,16,320]{2,1,0:T(8,128)S(1)}, u32[]{:S(2)}, u32[]{:S(2)}) collective-permute-start(f32[2,16,320]{2,1,0:T(8,128)} %get-tuple-element.69), channel_id=1, source_target_pairs={{0,1},{1,2},{2,3},{3,4},{4,5},{5,6},{6,7},{7,8},{8,9},{9,10},{10,1... | collective-permute-start | bytes 122888 | tf_op jit(solution)/shard_map/ppermute | solution.py:139
  80.7 16.8 %collective-permute-start.23 = (f32[2,16,320]{2,1,0:T(8,128)}, f32[2,16,320]{2,1,0:T(8,128)}, u32[]{:S(2)}, u32[]{:S(2)}) collective-permute-start(f32[2,16,320]{2,1,0:T(8,128)} %get-tuple-element.70), channel_id=1, source_target_pairs={{0,31},{1,0},{2,1},{3,2},{4,3},{5,4},{6,5},{7,6},{8,7},{9,8},{10,9... | collective-permute-start | bytes 122888 | tf_op jit(solution)/shard_map/ppermute | solution.py:139
  85.5 12.1 %collective-permute-start.21 = (f32[2,16,320]{2,1,0:T(8,128)S(1)}, f32[2,16,320]{2,1,0:T(8,128)}, u32[]{:S(2)}, u32[]{:S(2)}) collective-permute-start(f32[2,16,320]{2,1,0:T(8,128)S(1)} %get-tuple-element.67.wall0.refs_10_), channel_id=1, source_target_pairs={{0,224},{32,0},{64,32},{96,64},{128,96},{160,128},{192,160},{224,1... | collective-permute-start | bytes 122888 | tf_op jit(solution)/shard_map/ppermute | solution.py:139
  87.9 9.6 %collective-permute-start.20 = (f32[2,16,320]{2,1,0:T(8,128)S(1)}, f32[2,16,320]{2,1,0:T(8,128)}, u32[]{:S(2)}, u32[]{:S(2)}) collective-permute-start(f32[2,16,320]{2,1,0:T(8,128)S(1)} %get-tuple-element.68.wall1.refs_11_), channel_id=1, source_target_pairs={{0,32},{32,64},{64,96},{96,128},{128,160},{160,192},{192,224},{224... | collective-permute-start | bytes 122888 | tf_op jit(solution)/shard_map/ppermute | solution.py:139
  88.7 37.1 %all-to-all-start.1 = ((f32[16,32,128]{2,1,0:T(8,128)}), f32[16,32,128]{2,1,0:T(8,128)S(1)}, u32[]{:S(2)}, u32[]{:S(2)}) async-start(f32[16,32,128]{2,1,0:T(8,128)} %resum.2), calls=%async_computation.1 | async-start | bytes 524288 | tf_op jit(solution)/shard_map/all_to_all | solution.py:245
  100.4 9.0 %collective-permute-start.26 = (f32[2,16,320]{2,1,0:T(8,128)S(1)}, f32[2,16,320]{2,1,0:T(8,128)S(1)}, u32[]{:S(2)}, u32[]{:S(2)}) collective-permute-start(f32[2,16,320]{2,1,0:T(8,128)S(1)} %get-tuple-element.73), channel_id=1, source_target_pairs={{0,1},{1,2},{2,3},{3,4},{4,5},{5,6},{6,7},{7,8},{8,9},{9,10},{10,1... | collective-permute-start | bytes 122888 | tf_op jit(solution)/shard_map/ppermute | solution.py:139
  101.8 7.6 %collective-permute-start.27 = (f32[2,16,320]{2,1,0:T(8,128)S(1)}, f32[2,16,320]{2,1,0:T(8,128)S(1)}, u32[]{:S(2)}, u32[]{:S(2)}) collective-permute-start(f32[2,16,320]{2,1,0:T(8,128)S(1)} %get-tuple-element.74), channel_id=1, source_target_pairs={{0,31},{1,0},{2,1},{3,2},{4,3},{5,4},{6,5},{7,6},{8,7},{9,8},{10,9... | collective-permute-start | bytes 122888 | tf_op jit(solution)/shard_map/ppermute | solution.py:139
  112.3 11.2 %collective-permute-start.30 = (f32[2,16,320]{2,1,0:T(8,128)S(1)}, f32[2,16,320]{2,1,0:T(8,128)S(1)}, u32[]{:S(2)}, u32[]{:S(2)}) collective-permute-start(f32[2,16,320]{2,1,0:T(8,128)S(1)} %get-tuple-element.77), channel_id=1, source_target_pairs={{0,1},{1,2},{2,3},{3,4},{4,5},{5,6},{6,7},{7,8},{8,9},{9,10},{10,1... | collective-permute-start | bytes 122888 | tf_op jit(solution)/shard_map/ppermute | solution.py:139
  112.7 10.9 %collective-permute-start.31 = (f32[2,16,320]{2,1,0:T(8,128)S(1)}, f32[2,16,320]{2,1,0:T(8,128)S(1)}, u32[]{:S(2)}, u32[]{:S(2)}) collective-permute-start(f32[2,16,320]{2,1,0:T(8,128)S(1)} %get-tuple-element.78), channel_id=1, source_target_pairs={{0,31},{1,0},{2,1},{3,2},{4,3},{5,4},{6,5},{7,6},{8,7},{9,8},{10,9... | collective-permute-start | bytes 122888 | tf_op jit(solution)/shard_map/ppermute | solution.py:139
  (32 other events, 212.8 us)
where the time goes:
time: 167 us; the launch traced here: 166 us
  starting transfers between devices  77.9 us (47%)
  Pallas kernels  40.5 us (24%)
  blocking collectives  32.4 us (19%)
  local copies, waits for them, and re-layouts  11.8 us (7%)
  waiting for transfers between devices  2.78 us (2%)
    ppermute x32, starting transfers between devices, ring(): lax.ppermute(array, axis, [(i, (i + step) % count) for i in range(count)])  66.5 us
    pallas_call x22, Pallas kernels, call(): pl.pallas_call(kernel, in_specs=in_specs or [VMEM] * len(operands), out_s...  36.5 us
    all_to_all x1, blocking collectives, device_sum(): return lax.all_to_all(copies, AXES, 0, 0, axis_index_groups=FAR)  17.4 us
    all_to_all x1, blocking collectives, device_sum(): received = lax.all_to_all(copies, AXES, 0, 0, axis_index_groups=NEAR)  15 us
    unnamed x44, local copies, waits for them, and re-layouts  11.8 us
    all_to_all x1, starting transfers between devices, device_sum(): received = lax.all_to_all(copies, AXES, 0, 0, axis_index_groups=NEAR)  6.49 us
    all_to_all x1, starting transfers between devices, device_sum(): return lax.all_to_all(copies, AXES, 0, 0, axis_index_groups=FAR)  4.96 us
    pallas_call x1, Pallas kernels, prepare(): pl.pallas_call(prepare_kernel, grid=(4,), in_specs=[pl.BlockSpec((1, 1, R...  3.98 us
  transfers between devices with their start and end apart: 34, of which 3 were waited for; matrix products, arithmetic and copies ran while one was open for 0% of the time, Pallas kernels for 15%

commit v1 on v0

v1 whole, which is shorter than its diff:
```python
import functools

import jax
import jax.numpy as jnp
from jax import lax
from jax.experimental import pallas as pl
from jax.experimental.pallas import tpu as pltpu
from jax.sharding import PartitionSpec as P

ROWS = 320
BLOCK = 16
STEPS = 4
PANEL = 80
INNER = PANEL - BLOCK
SPAN = 2 * STEPS + 1
basis_shift = 1.5
basis_scale = 0.8

f32 = jnp.float32
bf16 = jnp.bfloat16
highest = lax.Precision.HIGHEST
AXES = ("wall", "stream")
NT = (((1,), (1,)), ((), ()))
VMEM = pl.BlockSpec(memory_space=pltpu.VMEM)
SMEM = pl.BlockSpec(memory_space=pltpu.SMEM)


def groups_by(key):
    found = {}
    for wall in range(8):
        for stream in range(32):
            place = key(wall // 2, wall % 2, stream % 4, stream // 4)
            found.setdefault(place, []).append(wall * 32 + stream)
    return list(found.values())


PLANE = groups_by(lambda x, core, y, z: (core, z))
DEPTH = groups_by(lambda x, core, y, z: (core, x, y))
SIBLING = [(w * 32 + r, (w ^ 1) * 32 + r) for w in range(8) for r in range(32)]
WIDTH = SPAN * BLOCK
PACKED = 96
GROWTH = 2.0**-4


def call(kernel, name, out_shape, operands, flops, in_specs=None):
    return pl.pallas_call(
        kernel,
        in_specs=in_specs or [VMEM] * len(operands),
        out_specs=jax.tree.map(lambda _: VMEM, out_shape),
        out_shape=out_shape,
        compiler_params=pltpu.CompilerParams(vmem_limit_bytes=8 * 2**20),
        cost_estimate=pl.CostEstimate(flops=flops, bytes_accessed=2**20, transcendentals=0),
        name=name,
    )(*operands)


def shape(*dims, dtype=f32):
    return jax.ShapeDtypeStruct(dims, dtype)


def split(value):
    high = value.astype(bf16)
    return high, (value - high.astype(f32)).astype(bf16)


def prepare_kernel(diag, coupling, local_high, local_low, far_high, far_low):
    element = pl.program_id(0)
    wall, stream = element // 2, element % 2
    row = lax.broadcasted_iota(jnp.int32, (ROWS, ROWS), 0)
    column = lax.broadcasted_iota(jnp.int32, (ROWS, ROWS), 1)

    def store(high, low, at, matrix):
        high_part, low_part = split(matrix * (1.0 / basis_scale))
        high[element, :, at * ROWS : (at + 1) * ROWS] = high_part
        low[element, :, at * ROWS : (at + 1) * ROWS] = low_part

    store(local_high, local_low, 0, diag[0, 0] - jnp.where(row == column, basis_shift, 0.0))
    store(local_high, local_low, 1, coupling[1 - wall, 0, 0])
    store(local_high, local_low, 2, coupling[3 - stream, 0, 0])
    store(far_high, far_low, 0, coupling[wall, 0, 0])
    store(far_high, far_low, 1, coupling[2 + stream, 0, 0])


def prepare(diag_blocks, coupling):
    return pl.pallas_call(
        prepare_kernel,
        grid=(4,),
        in_specs=[
            pl.BlockSpec((1, 1, ROWS, ROWS), lambda e: (e // 2, e % 2, 0, 0)),
            pl.BlockSpec((4, 1, 1, ROWS, ROWS), lambda e: (0, e // 2, e % 2, 0, 0)),
        ],
        out_specs=[VMEM] * 4,
        out_shape=[shape(4, ROWS, 3 * ROWS, dtype=bf16)] * 2
        + [shape(4, ROWS, 2 * ROWS, dtype=bf16)] * 2,
        compiler_params=pltpu.CompilerParams(vmem_limit_bytes=32 * 2**20),
        cost_estimate=pl.CostEstimate(flops=0, bytes_accessed=2**24, transcendentals=0),
        name="prepare",
    )(
        pltpu.with_memory_space_constraint(diag_blocks, pltpu.HBM),
        pltpu.with_memory_space_constraint(coupling, pltpu.HBM),
    )


def times(high, low, sources):
    highs, lows = zip(*[split(source) for source in sources])
    high_source = jnp.concatenate(highs, axis=1)
    both = jnp.concatenate([high_source, jnp.concatenate(lows, axis=1)], axis=0)
    first = lax.dot_general(both, high, NT, preferred_element_type=f32)
    second = lax.dot_general(high_source, low, NT, preferred_element_type=f32)
    return first[:BLOCK] + (first[BLOCK:] + second)


def gram_row(powers):
    panels = element_panels(powers)
    return sum(
        lax.dot_general(
            panel[-BLOCK:], panel, NT, precision=highest, preferred_element_type=f32
        )
        for panel in panels
    )


def local_kernel(high, low, *refs):
    powers, (partial, row) = refs[:-2], refs[-2:]
    field = powers[-2:]
    for w in range(2):
        for s in range(2):
            sources = [field[w][s], field[1 - w][s], field[w][1 - s]]
            partial[w, s] = times(high[2 * w + s], low[2 * w + s], sources)
    row[...] = gram_row(powers)


def far_kernel(scale, inside, partial, below, above, before, behind, high, low, *faces):
    wall_side, stream_side = (below, above), (before, behind)
    for w in range(2):
        for s in range(2):
            sources = [
                jnp.where(inside[w] > 0, wall_side[w][s], 0.0),
                jnp.where(inside[2 + s] > 0, stream_side[s][w], 0.0),
            ]
            value = partial[w, s] + times(high[2 * w + s], low[2 * w + s], sources)
            if scale != 1.0:
                value = value * scale
            faces[w][s] = value
            faces[2 + s][w] = value


def start_kernel(forcing, *faces):
    for w in range(2):
        for s in range(2):
            value = forcing[:, w, s, :]
            faces[w][s] = value
            faces[2 + s][w] = value


FACES = [shape(2, BLOCK, ROWS)] * 4


def ring(array, axis, step):
    count = lax.axis_size(axis)
    return lax.ppermute(array, axis, [(i, (i + step) % count) for i in range(count)])


def advance(faces, powers, parts, inside, scale):
    wall0, wall1, stream0, stream1 = faces
    below, above = ring(wall1, "wall", 1), ring(wall0, "wall", -1)
    before, behind = ring(stream1, "stream", 1), ring(stream0, "stream", -1)
    local_high, local_low, far_high, far_low = parts
    partial, row = call(
        local_kernel,
        "local",
        [shape(2, 2, BLOCK, ROWS), shape(BLOCK, 8 * len(powers))],
        (local_high, local_low, *powers),
        10**9,
    )
    faces = call(
        functools.partial(far_kernel, scale),
        "far",
        FACES,
        (inside, partial, below, above, before, behind, far_high, far_low),
        10**9,
        in_specs=[SMEM] + [VMEM] * 7,
    )
    return faces, row


def pack_kernel(inside, *refs):
    rows, powers, (keep, send) = refs[: SPAN - 1], refs[SPAN - 1 : -2], refs[-2:]
    lines = [row[...] for row in rows] + [gram_row(powers)]
    last = lines[8]
    first_half = jnp.concatenate(
        [last[:, :128], lines[7], jnp.concatenate([lines[6], lines[0]], axis=1)], axis=0
    )
    second_half = jnp.concatenate(
        [
            jnp.concatenate([lines[5], lines[1]], axis=1),
            jnp.concatenate([lines[4], lines[2]], axis=1),
            jnp.concatenate([lines[3], last[:, 128:], jnp.zeros((BLOCK, 48), f32)], axis=1),
        ],
        axis=0,
    )
    core = inside[4] > 0
    keep[...] = jnp.where(core, second_half, first_half)
    send[...] = jnp.where(core, first_half, second_half)


def unpack_gram(first, second):
    lines = [
        first[32:48, 112:],
        second[:16, 96:],
        second[16:32, 80:],
        second[32:48, :64],
        second[16:32, :80],
        second[:16, :96],
        first[32:48, :112],
        first[16:32],
        jnp.concatenate([first[:16], second[32:48, 64:80]], axis=1),
    ]
    lower = jnp.concatenate(
        [
            line
            if line.shape[1] == WIDTH
            else jnp.concatenate([line, jnp.zeros((BLOCK, WIDTH - line.shape[1]), f32)], axis=1)
            for line in lines
        ],
        axis=0,
    )
    row = lax.broadcasted_iota(jnp.int32, (WIDTH, WIDTH), 0) // BLOCK
    column = lax.broadcasted_iota(jnp.int32, (WIDTH, WIDTH), 1) // BLOCK
    return jnp.where(row >= column, lower, lower.T)


def small_solve(gram):
    right = basis_shift * gram[:, :INNER] + basis_scale * gram[:, BLOCK:]
    normal = basis_shift * right[:INNER] + basis_scale * right[BLOCK:]
    target = basis_shift * gram[:INNER, :BLOCK] + basis_scale * gram[BLOCK:, :BLOCK]
    system = jnp.concatenate([normal, target, jnp.zeros((INNER, 48), f32)], axis=1)
    rows = lax.broadcasted_iota(jnp.int32, (INNER, 128), 0)
    group = 4
    for start in range(0, INNER, group):
        columns = [
            jnp.broadcast_to(system[:, start + j : start + j + 1], (INNER, 128))
            for j in range(group)
        ]
        for j in range(group):
            k = start + j
            inverse = 1.0 / columns[j][k : k + 1]
            pivot_row = system[k : k + 1] * inverse
            system = jnp.where(rows == k, pivot_row, system - columns[j] * pivot_row)
            for later in range(j + 1, group):
                scaled = columns[later][k : k + 1] * inverse
                columns[later] = jnp.where(
                    rows == k, scaled, columns[later] - columns[j] * scaled
                )
    coefficients = system[:, INNER:PANEL]
    zero = jnp.zeros((BLOCK, BLOCK), f32)
    update = basis_shift * jnp.concatenate([coefficients, zero], axis=0)
    update = update + basis_scale * jnp.concatenate([zero, coefficients], axis=0)
    return coefficients, update


def element_panels(powers):
    count = len(powers) // 2
    return [
        jnp.concatenate([powers[2 * j + w][s] for j in range(count)], axis=0)
        for w in range(2)
        for s in range(2)
    ]


def add_spread_kernel(own, other, copies):
    copies[...] = jnp.broadcast_to((own[...] + other[...])[None], copies.shape)


def sum_spread_kernel(received, copies):
    copies[...] = jnp.broadcast_to(jnp.sum(received[...], axis=0)[None], copies.shape)


def sum_kernel(received, total):
    total[...] = jnp.sum(received[...], axis=0)


def device_sum(keep, send):
    half = PACKED // 2
    other = lax.ppermute(send, AXES, SIBLING)
    copies = call(add_spread_kernel, "join", shape(16, half, 128), (keep, other), 10**6)
    received = lax.all_to_all(copies, AXES, 0, 0, axis_index_groups=PLANE)
    copies = call(sum_spread_kernel, "resum", shape(8, half, 128), (received,), 10**6)
    received = lax.all_to_all(copies, AXES, 0, 0, axis_index_groups=DEPTH)
    total = call(sum_kernel, "sum", shape(half, 128), (received,), 10**6)
    return total, lax.ppermute(total, AXES, SIBLING)


def dot(left, right, dims=(((1,), (0,)), ((), ()))):
    return lax.dot_general(left, right, dims, precision=highest, preferred_element_type=f32)


def finish_kernel(inside, own, other, *refs):
    powers, (solution_out, residual_out) = refs[:-2], refs[-2:]
    core = inside[4] > 0
    own, other = own[...], other[...]
    gram = unpack_gram(jnp.where(core, other, own), jnp.where(core, own, other))
    coefficients, update = small_solve(gram[:PANEL, :PANEL])
    row = lax.broadcasted_iota(jnp.int32, (BLOCK, PANEL), 0)
    column = lax.broadcasted_iota(jnp.int32, (BLOCK, PANEL), 1)
    identity = jnp.where(row == column, 1.0, 0.0)
    remainder = identity - update.T
    zeros = lambda width: [jnp.zeros((BLOCK, width), f32)] if width else []
    mixing = jnp.concatenate(
        [
            jnp.concatenate(
                zeros(BLOCK * j) + [remainder] + zeros(WIDTH - PANEL - BLOCK * j), axis=1
            )
            for j in range(STEPS + 1)
        ],
        axis=0,
    )
    power = lax.broadcasted_iota(jnp.int32, (PANEL, WIDTH), 1) // BLOCK
    for j in range(STEPS + 1, SPAN):
        mixing = jnp.where(power == j, mixing * GROWTH ** (STEPS - j), mixing)
    second_gram = dot(dot(mixing, gram), mixing, NT)
    second_coefficients, second_update = small_solve(second_gram)
    first_weights = jnp.concatenate([coefficients.T] + zeros(WIDTH - INNER), axis=1)
    second = jnp.concatenate(
        [
            jnp.concatenate([second_coefficients.T] + zeros(BLOCK), axis=1),
            identity - second_update.T,
        ],
        axis=0,
    )
    weights = dot(second, mixing)
    weights = jnp.concatenate([weights[:BLOCK] + first_weights, weights[BLOCK:]], axis=0)
    for e, panel in enumerate(element_panels(powers)):
        mixed = dot(weights, panel)
        solution_out[:, e // 2, e % 2, :] = mixed[:BLOCK]
        residual_out[:, e // 2, e % 2, :] = mixed[BLOCK:]


def on_device(forcing, diag_blocks, coupling):
    wall, stream = lax.axis_index("wall"), lax.axis_index("stream")
    inside = jnp.stack([wall > 0, wall < 7, stream > 0, stream < 31, wall % 2 > 0])
    inside = inside.astype(jnp.int32)
    faces = call(start_kernel, "start", FACES, (forcing,), 10**6)
    parts = prepare(diag_blocks, coupling)
    powers = [*faces[:2]]
    rows = []
    for step in range(2 * STEPS):
        scale = 1.0 if step < STEPS else GROWTH
        faces, row = advance(faces, powers, parts, inside, scale)
        powers += faces[:2]
        rows.append(row)
    keep, send = call(
        pack_kernel,
        "pack",
        [shape(PACKED // 2, 128)] * 2,
        (inside, *rows, *powers),
        10**7,
        in_specs=[SMEM] + [VMEM] * (len(rows) + len(powers)),
    )
    own, other = device_sum(keep, send)
    return call(
        finish_kernel,
        "finish",
        [shape(BLOCK, 2, 2, ROWS)] * 2,
        (inside, own, other, *powers),
        10**8,
        in_specs=[SMEM] + [VMEM] * (2 + len(powers)),
    )


def solution(mesh):
    return jax.shard_map(
        on_device,
        mesh=mesh,
        in_specs=(
            P(None, "wall", "stream", None),
            P("wall", "stream", None, None),
            P(None, "wall", "stream", None, None),
        ),
        out_specs=(P(None, "wall", "stream", None), P(None, "wall", "stream", None)),
        check_vma=False,
    )
```

time: 167 us -> 153 us (0.916)
  blocking collectives: 32.4 us -> 25.2 us
  local copies, waits for them, and re-layouts: 11.8 us -> 5.56 us
  starting transfers between devices: 77.9 us -> 72.6 us
  Pallas kernels: 40.5 us -> 44.9 us
    all_to_all x2 -> x0, starting transfers between devices: 11.5 us -> none  [the longest x1 6.49 us: device_sum(): received = lax.all_to_all(copies, AXES, 0, 0, axis_index_groups=NEAR)]
    all_to_all x2, blocking collectives: 32.4 us -> 25.2 us  [the longest x1 13.3 us: device_sum(): received = lax.all_to_all(copies, AXES, 0, 0, axis_index_groups=DEPTH)]
    unnamed x44 -> x14, local copies, waits for them, and re-layouts: 11.8 us -> 5.46 us
    ppermute x0 -> x2, starting transfers between devices: none -> 5.37 us  [the longest x1 2.97 us: device_sum(): return (total, lax.ppermute(total, AXES, SIBLING))]
    pallas_call x1, Pallas kernels: 3.98 us -> 6.28 us  [prepare(): pl.pallas_call(prepare_kernel, grid=(4,), in_specs=[pl.BlockSpec((1, 1, R...]
    pallas_call x22, Pallas kernels: 36.5 us -> 38.6 us  [call(): pl.pallas_call(kernel, in_specs=in_specs or [VMEM] * len(operands), out_s...]
    ppermute x0 -> x2, waiting for transfers between devices: none -> 1.7 us  [the longest x1 0.85 us: device_sum(): other = lax.ppermute(send, AXES, SIBLING)]
  transfers between devices with their start and end apart: 34 -> 34, of which waited for: 3 -> 3; matrix products, arithmetic and copies ran while one was open for 0% -> 0% of each run, Pallas kernels for 15% -> 14%
where the time goes in v1:
time: 153 us; the launch traced here: 152 us
  starting transfers between devices  72.6 us (47%)
  Pallas kernels  44.9 us (29%)
  blocking collectives  25.2 us (16%)
  local copies, waits for them, and re-layouts  5.56 us (4%)
  waiting for transfers between devices  3 us (2%)
    ppermute x32, starting transfers between devices, ring(): lax.ppermute(array, axis, [(i, (i + step) % count) for i in range(count)])  67.2 us
    pallas_call x22, Pallas kernels, call(): pl.pallas_call(kernel, in_specs=in_specs or [VMEM] * len(operands), out_s...  38.6 us
    all_to_all x1, blocking collectives, device_sum(): received = lax.all_to_all(copies, AXES, 0, 0, axis_index_groups=DEPTH)  13.3 us
    all_to_all x1, blocking collectives, device_sum(): received = lax.all_to_all(copies, AXES, 0, 0, axis_index_groups=PLANE)  11.9 us
    pallas_call x1, Pallas kernels, prepare(): pl.pallas_call(prepare_kernel, grid=(4,), in_specs=[pl.BlockSpec((1, 1, R...  6.28 us
    unnamed x14, local copies, waits for them, and re-layouts  5.46 us
  transfers between devices with their start and end apart: 34, of which 3 were waited for; matrix products, arithmetic and copies ran while one was open for 0% of the time, Pallas kernels for 14%

profile of v1, /device:TPU:1, one launch (start us, length us, event | category | flops | bytes accessed | tf_op | source)
XLA Modules:
  0.0 152.3 jit_solution(18246808331468715403)
XLA Ops:
  1.6 2.2 %collective-permute-start.2 = (f32[2,16,320]{2,1,0:T(8,128)S(1)}, f32[2,16,320]{2,1,0:T(8,128)S(1)}, u32[]{:S(2)}, u32[]{:S(2)}) collective-permute-start(f32[2,16,320]{2,1,0:T(8,128)S(1)} %get-tuple-element.64), channel_id=1, source_target_pairs={{0,1},{1,2},{2,3},{3,4},{4,5},{5,6},{6,7},{7,8},{8,9},{9,10},{10,1... | collective-permute-start | bytes 122888 | tf_op jit(solution)/shard_map/ppermute | solution.py:161
  3.8 6.8 %collective-permute-start.3 = (f32[2,16,320]{2,1,0:T(8,128)S(1)}, f32[2,16,320]{2,1,0:T(8,128)S(1)}, u32[]{:S(2)}, u32[]{:S(2)}) collective-permute-start(f32[2,16,320]{2,1,0:T(8,128)S(1)} %get-tuple-element.65), channel_id=1, source_target_pairs={{0,31},{1,0},{2,1},{3,2},{4,3},{5,4},{6,5},{7,6},{8,7},{9,8},{10,9... | collective-permute-start | bytes 122888 | tf_op jit(solution)/shard_map/ppermute | solution.py:161
  12.6 6.3 %prepare.1 = (bf16[4,320,960]{2,1,0:T(8,128)(2,1)S(1)}, bf16[4,320,960]{2,1,0:T(8,128)(2,1)S(1)}, bf16[4,320,640]{2,1,0:T(8,128)(2,1)S(1)}, bf16[4,320,640]{2,1,0:T(8,128)(2,1)S(1)}) custom-call(f32[2,2,320,320]{3,2,1,0:T(8,128)} %diag.1, f32[4,2,2,320,320]{4,3,2,1,0:T(8,128)} %coupling.1), custom_call_target="tpu_custom_call" | custom-call | bytes 16777216 | tf_op jit(solution)/shard_map/prepare/pallas_call | solution.py:85
  26.9 4.8 %collective-permute-start.7 = (f32[2,16,320]{2,1,0:T(8,128)S(1)}, f32[2,16,320]{2,1,0:T(8,128)S(1)}, u32[]{:S(2)}, u32[]{:S(2)}) collective-permute-start(f32[2,16,320]{2,1,0:T(8,128)S(1)} %get-tuple-element.73), channel_id=1, source_target_pairs={{0,31},{1,0},{2,1},{3,2},{4,3},{5,4},{6,5},{7,6},{8,7},{9,8},{10,9... | collective-permute-start | bytes 122888 | tf_op jit(solution)/shard_map/ppermute | solution.py:161
  37.8 4.8 %collective-permute-start.11 = (f32[2,16,320]{2,1,0:T(8,128)S(1)}, f32[2,16,320]{2,1,0:T(8,128)S(1)}, u32[]{:S(2)}, u32[]{:S(2)}) collective-permute-start(f32[2,16,320]{2,1,0:T(8,128)S(1)} %get-tuple-element.79), channel_id=1, source_target_pairs={{0,31},{1,0},{2,1},{3,2},{4,3},{5,4},{6,5},{7,6},{8,7},{9,8},{10,9... | collective-permute-start | bytes 122888 | tf_op jit(solution)/shard_map/ppermute | solution.py:161
  42.6 4.6 %collective-permute-start.9 = (f32[2,16,320]{2,1,0:T(8,128)S(1)}, f32[2,16,320]{2,1,0:T(8,128)S(1)}, u32[]{:S(2)}, u32[]{:S(2)}) collective-permute-start(f32[2,16,320]{2,1,0:T(8,128)S(1)} %get-tuple-element.74.refs_4_.refs_12_), channel_id=1, source_target_pairs={{0,224},{32,0},{64,32},{96,64},{128,96},{160,128},{192,160},{224,1... | collective-permute-start | bytes 122888 | tf_op jit(solution)/shard_map/ppermute | solution.py:161
  50.6 4.8 %collective-permute-start.15 = (f32[2,16,320]{2,1,0:T(8,128)S(1)}, f32[2,16,320]{2,1,0:T(8,128)S(1)}, u32[]{:S(2)}, u32[]{:S(2)}) collective-permute-start(f32[2,16,320]{2,1,0:T(8,128)S(1)} %get-tuple-element.85), channel_id=1, source_target_pairs={{0,31},{1,0},{2,1},{3,2},{4,3},{5,4},{6,5},{7,6},{8,7},{9,8},{10,9... | collective-permute-start | bytes 122888 | tf_op jit(solution)/shard_map/ppermute | solution.py:161
  55.4 3.4 %collective-permute-start.13 = (f32[2,16,320]{2,1,0:T(8,128)S(1)}, f32[2,16,320]{2,1,0:T(8,128)S(1)}, u32[]{:S(2)}, u32[]{:S(2)}) collective-permute-start(f32[2,16,320]{2,1,0:T(8,128)S(1)} %get-tuple-element.80.refs_6_.refs_14_), channel_id=1, source_target_pairs={{0,224},{32,0},{64,32},{96,64},{128,96},{160,128},{192,160},{224,1... | collective-permute-start | bytes 122888 | tf_op jit(solution)/shard_map/ppermute | solution.py:161
  62.4 4.8 %collective-permute-start.19 = (f32[2,16,320]{2,1,0:T(8,128)S(1)}, f32[2,16,320]{2,1,0:T(8,128)S(1)}, u32[]{:S(2)}, u32[]{:S(2)}) collective-permute-start(f32[2,16,320]{2,1,0:T(8,128)S(1)} %get-tuple-element.91), channel_id=1, source_target_pairs={{0,31},{1,0},{2,1},{3,2},{4,3},{5,4},{6,5},{7,6},{8,7},{9,8},{10,9... | collective-permute-start | bytes 122888 | tf_op jit(solution)/shard_map/ppermute | solution.py:161
  67.2 3.3 %collective-permute-start.17 = (f32[2,16,320]{2,1,0:T(8,128)S(1)}, f32[2,16,320]{2,1,0:T(8,128)S(1)}, u32[]{:S(2)}, u32[]{:S(2)}) collective-permute-start(f32[2,16,320]{2,1,0:T(8,128)S(1)} %get-tuple-element.86.refs_8_.refs_16_), channel_id=1, source_target_pairs={{0,224},{32,0},{64,32},{96,64},{128,96},{160,128},{192,160},{224,1... | collective-permute-start | bytes 122888 | tf_op jit(solution)/shard_map/ppermute | solution.py:161
  74.2 4.8 %collective-permute-start.23 = (f32[2,16,320]{2,1,0:T(8,128)S(1)}, f32[2,16,320]{2,1,0:T(8,128)S(1)}, u32[]{:S(2)}, u32[]{:S(2)}) collective-permute-start(f32[2,16,320]{2,1,0:T(8,128)S(1)} %get-tuple-element.97), channel_id=1, source_target_pairs={{0,31},{1,0},{2,1},{3,2},{4,3},{5,4},{6,5},{7,6},{8,7},{9,8},{10,9... | collective-permute-start | bytes 122888 | tf_op jit(solution)/shard_map/ppermute | solution.py:161
  79.0 3.2 %collective-permute-start.21 = (f32[2,16,320]{2,1,0:T(8,128)S(1)}, f32[2,16,320]{2,1,0:T(8,128)S(1)}, u32[]{:S(2)}, u32[]{:S(2)}) collective-permute-start(f32[2,16,320]{2,1,0:T(8,128)S(1)} %get-tuple-element.92.refs_10_.refs_18_), channel_id=1, source_target_pairs={{0,224},{32,0},{64,32},{96,64},{128,96},{160,128},{192,160},{224,1... | collective-permute-start | bytes 122888 | tf_op jit(solution)/shard_map/ppermute | solution.py:161
  86.0 4.8 %collective-permute-start.27 = (f32[2,16,320]{2,1,0:T(8,128)S(1)}, f32[2,16,320]{2,1,0:T(8,128)S(1)}, u32[]{:S(2)}, u32[]{:S(2)}) collective-permute-start(f32[2,16,320]{2,1,0:T(8,128)S(1)} %get-tuple-element.103), channel_id=1, source_target_pairs={{0,31},{1,0},{2,1},{3,2},{4,3},{5,4},{6,5},{7,6},{8,7},{9,8},{10,9... | collective-permute-start | bytes 122888 | tf_op jit(solution)/shard_map/ppermute | solution.py:161
  90.8 3.1 %collective-permute-start.25 = (f32[2,16,320]{2,1,0:T(8,128)S(1)}, f32[2,16,320]{2,1,0:T(8,128)S(1)}, u32[]{:S(2)}, u32[]{:S(2)}) collective-permute-start(f32[2,16,320]{2,1,0:T(8,128)S(1)} %get-tuple-element.98.refs_12_.refs_20_), channel_id=1, source_target_pairs={{0,224},{32,0},{64,32},{96,64},{128,96},{160,128},{192,160},{224,1... | collective-permute-start | bytes 122888 | tf_op jit(solution)/shard_map/ppermute | solution.py:161
  93.9 2.2 %local.14 = (f32[2,2,16,320]{3,2,1,0:T(8,128)S(1)}, f32[16,112]{1,0:T(8,128)S(1)}) custom-call(bf16[4,320,960]{2,1,0:T(8,128)(2,1)S(1)} %get-tuple-element.58.high, bf16[4,320,960]{2,1,0:T(8,128)(2,1)S(1)} %copy-done.1, f32[2,16,320]{2,1,0:T(8,128)S(1)} %get-tuple-element.60.refs_0_.refs_8_, f32[2,16,320]{2,1,0:T(8,128)S(1)} %get-tuple-element.61.refs_1_.refs_9_, ...), custom_call_target="tpu_custom_call" | custom-call | flops 1000000000 | bytes 1048576 | tf_op jit(solution)/shard_map/local/pallas_call | solution.py:46
  97.8 4.8 %collective-permute-start.31 = (f32[2,16,320]{2,1,0:T(8,128)S(1)}, f32[2,16,320]{2,1,0:T(8,128)S(1)}, u32[]{:S(2)}, u32[]{:S(2)}) collective-permute-start(f32[2,16,320]{2,1,0:T(8,128)S(1)} %get-tuple-element.109), channel_id=1, source_target_pairs={{0,31},{1,0},{2,1},{3,2},{4,3},{5,4},{6,5},{7,6},{8,7},{9,8},{10,9... | collective-permute-start | bytes 122888 | tf_op jit(solution)/shard_map/ppermute | solution.py:161
  102.6 3.0 %collective-permute-start.29 = (f32[2,16,320]{2,1,0:T(8,128)S(1)}, f32[2,16,320]{2,1,0:T(8,128)S(1)}, u32[]{:S(2)}, u32[]{:S(2)}) collective-permute-start(f32[2,16,320]{2,1,0:T(8,128)S(1)} %get-tuple-element.104.refs_14_.refs_22_), channel_id=1, source_target_pairs={{0,224},{32,0},{64,32},{96,64},{128,96},{160,128},{192,160},{224,1... | collective-permute-start | bytes 122888 | tf_op jit(solution)/shard_map/ppermute | solution.py:161
  105.6 2.3 %local.15 = (f32[2,2,16,320]{3,2,1,0:T(8,128)S(1)}, f32[16,128]{1,0:T(8,128)S(1)}) custom-call(bf16[4,320,960]{2,1,0:T(8,128)(2,1)S(1)} %get-tuple-element.58.high, bf16[4,320,960]{2,1,0:T(8,128)(2,1)S(1)} %copy-done.1, f32[2,16,320]{2,1,0:T(8,128)S(1)} %get-tuple-element.60.refs_0_.refs_8_, f32[2,16,320]{2,1,0:T(8,128)S(1)} %get-tuple-element.61.refs_1_.refs_9_, ...), custom_call_target="tpu_custom_call" | custom-call | flops 1000000000 | bytes 1048576 | tf_op jit(solution)/shard_map/local/pallas_call | solution.py:46
  108.0 2.2 %far.15 = (f32[2,16,320]{2,1,0:T(8,128)S(1)}, f32[2,16,320]{2,1,0:T(8,128)S(1)}, f32[2,16,320]{2,1,0:T(8,128)}, f32[2,16,320]{2,1,0:T(8,128)}) custom-call(s32[5]{0:T(128)S(1)} %convert_element_type.3.inside, f32[2,2,16,320]{3,2,1,0:T(8,128)S(1)} %get-tuple-element.107.partial, f32[2,16,320]{2,1,0:T(8,128)S(1)} %collective-permute-done.28.below, ...), custom_call_target="tpu_custom_call" | custom-call | flops 1000000000 | bytes 1048576 | tf_op jit(solution)/shard_map/far/pallas_call | solution.py:46
  111.8 2.4 %collective-permute-start.32 = (f32[48,128]{1,0:T(8,128)S(1)}, f32[48,128]{1,0:T(8,128)S(1)}, u32[]{:S(2)}, u32[]{:S(2)}) collective-permute-start(f32[48,128]{1,0:T(8,128)S(1)} %get-tuple-element.113), channel_id=1, source_target_pairs={{0,32},{1,33},{2,34},{3,35},{4,36},{5,37},{6,38},{7,39},{8,40},{9,... | collective-permute-start | bytes 73736 | tf_op jit(solution)/shard_map/ppermute | solution.py:285
  115.1 11.9 %all_to_all.10.received = f32[16,48,128]{2,1,0:T(8,128)S(1)} all-to-all(f32[16,48,128]{2,1,0:T(8,128)S(1)} %join.1), channel_id=1, replica_groups={{0,1,2,3,64,65,66,67,128,129,130,131,192,193,194,195},{4,5,6,7,68,69,70..., dimensions={0} | all-to-all | bytes 786432 | tf_op jit(solution)/shard_map/all_to_all | solution.py:287
  127.1 13.3 %all_to_all.11.received = f32[8,48,128]{2,1,0:T(8,128)S(1)} all-to-all(f32[8,48,128]{2,1,0:T(8,128)S(1)} %resum.1), channel_id=1, replica_groups={{0,4,8,12,16,20,24,28},{1,5,9,13,17,21,25,29},{2,6,10,14,18,22,26,30},{..., dimensions={0} | all-to-all | bytes 393216 | tf_op jit(solution)/shard_map/all_to_all | solution.py:289
  140.4 3.0 %collective-permute-start.33 = (f32[48,128]{1,0:T(8,128)S(1)}, f32[48,128]{1,0:T(8,128)S(1)}, u32[]{:S(2)}, u32[]{:S(2)}) collective-permute-start(f32[48,128]{1,0:T(8,128)S(1)} %sum.1.own), channel_id=1, source_target_pairs={{0,32},{1,33},{2,34},{3,35},{4,36},{5,37},{6,38},{7,39},{8,40},{9,... | collective-permute-start | bytes 73736 | tf_op jit(solution)/shard_map/ppermute | solution.py:291
  144.2 8.1 %finish.1 = (f32[16,2,2,320]{3,2,1,0:T(2,128)}, f32[16,2,2,320]{3,2,1,0:T(2,128)}) custom-call(s32[5]{0:T(128)S(1)} %convert_element_type.3.inside, f32[48,128]{1,0:T(8,128)S(1)} %sum.1.own, f32[48,128]{1,0:T(8,128)S(1)} %collective-permute-done.33.other, f32[2,16,320]{2,1,0:T(8,128)S(1)} %get-tuple-element.60.refs_0_.refs_8_, ...), custom_call_target="tpu_custom_call" | custom-call | flops 100000000 | bytes 1048576 | tf_op jit(solution)/shard_map/finish/pallas_call | solution.py:46
  (85 shorter events, 36.5 us)
Async XLA Ops:
  1.6 20.7 %collective-permute-start.2 = (f32[2,16,320]{2,1,0:T(8,128)S(1)}, f32[2,16,320]{2,1,0:T(8,128)S(1)}, u32[]{:S(2)}, u32[]{:S(2)}) collective-permute-start(f32[2,16,320]{2,1,0:T(8,128)S(1)} %get-tuple-element.64), channel_id=1, source_target_pairs={{0,1},{1,2},{2,3},{3,4},{4,5},{5,6},{6,7},{7,8},{8,9},{9,10},{10,1... | collective-permute-start | bytes 122888 | tf_op jit(solution)/shard_map/ppermute | solution.py:161
  3.8 18.5 %collective-permute-start.3 = (f32[2,16,320]{2,1,0:T(8,128)S(1)}, f32[2,16,320]{2,1,0:T(8,128)S(1)}, u32[]{:S(2)}, u32[]{:S(2)}) collective-permute-start(f32[2,16,320]{2,1,0:T(8,128)S(1)} %get-tuple-element.65), channel_id=1, source_target_pairs={{0,31},{1,0},{2,1},{3,2},{4,3},{5,4},{6,5},{7,6},{8,7},{9,8},{10,9... | collective-permute-start | bytes 122888 | tf_op jit(solution)/shard_map/ppermute | solution.py:161
  10.6 11.7 %collective-permute-start.1 = (f32[2,16,320]{2,1,0:T(8,128)S(1)}, f32[2,16,320]{2,1,0:T(8,128)S(1)}, u32[]{:S(2)}, u32[]{:S(2)}) collective-permute-start(f32[2,16,320]{2,1,0:T(8,128)S(1)} %get-tuple-element.60.refs_0_.refs_8_), channel_id=1, source_target_pairs={{0,224},{32,0},{64,32},{96,64},{128,96},{160,128},{192,160},{224,1... | collective-permute-start | bytes 122888 | tf_op jit(solution)/shard_map/ppermute | solution.py:161
  11.5 10.8 %collective-permute-start = (f32[2,16,320]{2,1,0:T(8,128)S(1)}, f32[2,16,320]{2,1,0:T(8,128)S(1)}, u32[]{:S(2)}, u32[]{:S(2)}) collective-permute-start(f32[2,16,320]{2,1,0:T(8,128)S(1)} %get-tuple-element.61.refs_1_.refs_9_), channel_id=1, source_target_pairs={{0,32},{32,64},{64,96},{96,128},{128,160},{160,192},{192,224},{224... | collective-permute-start | bytes 122888 | tf_op jit(solution)/shard_map/ppermute | solution.py:161
  26.9 8.3 %collective-permute-start.6 = (f32[2,16,320]{2,1,0:T(8,128)S(1)}, f32[2,16,320]{2,1,0:T(8,128)S(1)}, u32[]{:S(2)}, u32[]{:S(2)}) collective-permute-start(f32[2,16,320]{2,1,0:T(8,128)S(1)} %get-tuple-element.72), channel_id=1, source_target_pairs={{0,1},{1,2},{2,3},{3,4},{4,5},{5,6},{6,7},{7,8},{8,9},{9,10},{10,1... | collective-permute-start | bytes 122888 | tf_op jit(solution)/shard_map/ppermute | solution.py:161
  26.9 8.2 %collective-permute-start.7 = (f32[2,16,320]{2,1,0:T(8,128)S(1)}, f32[2,16,320]{2,1,0:T(8,128)S(1)}, u32[]{:S(2)}, u32[]{:S(2)}) collective-permute-start(f32[2,16,320]{2,1,0:T(8,128)S(1)} %get-tuple-element.73), channel_id=1, source_target_pairs={{0,31},{1,0},{2,1},{3,2},{4,3},{5,4},{6,5},{7,6},{8,7},{9,8},{10,9... | collective-permute-start | bytes 122888 | tf_op jit(solution)/shard_map/ppermute | solution.py:161
  37.8 11.2 %collective-permute-start.10 = (f32[2,16,320]{2,1,0:T(8,128)S(1)}, f32[2,16,320]{2,1,0:T(8,128)S(1)}, u32[]{:S(2)}, u32[]{:S(2)}) collective-permute-start(f32[2,16,320]{2,1,0:T(8,128)S(1)} %get-tuple-element.78), channel_id=1, source_target_pairs={{0,1},{1,2},{2,3},{3,4},{4,5},{5,6},{6,7},{7,8},{8,9},{9,10},{10,1... | collective-permute-start | bytes 122888 | tf_op jit(solution)/shard_map/ppermute | solution.py:161
  37.8 11.2 %collective-permute-start.11 = (f32[2,16,320]{2,1,0:T(8,128)S(1)}, f32[2,16,320]{2,1,0:T(8,128)S(1)}, u32[]{:S(2)}, u32[]{:S(2)}) collective-permute-start(f32[2,16,320]{2,1,0:T(8,128)S(1)} %get-tuple-element.79), channel_id=1, source_target_pairs={{0,31},{1,0},{2,1},{3,2},{4,3},{5,4},{6,5},{7,6},{8,7},{9,8},{10,9... | collective-permute-start | bytes 122888 | tf_op jit(solution)/shard_map/ppermute | solution.py:161
  42.6 6.4 %collective-permute-start.9 = (f32[2,16,320]{2,1,0:T(8,128)S(1)}, f32[2,16,320]{2,1,0:T(8,128)S(1)}, u32[]{:S(2)}, u32[]{:S(2)}) collective-permute-start(f32[2,16,320]{2,1,0:T(8,128)S(1)} %get-tuple-element.74.refs_4_.refs_12_), channel_id=1, source_target_pairs={{0,224},{32,0},{64,32},{96,64},{128,96},{160,128},{192,160},{224,1... | collective-permute-start | bytes 122888 | tf_op jit(solution)/shard_map/ppermute | solution.py:161
  50.6 10.1 %collective-permute-start.14 = (f32[2,16,320]{2,1,0:T(8,128)S(1)}, f32[2,16,320]{2,1,0:T(8,128)S(1)}, u32[]{:S(2)}, u32[]{:S(2)}) collective-permute-start(f32[2,16,320]{2,1,0:T(8,128)S(1)} %get-tuple-element.84), channel_id=1, source_target_pairs={{0,1},{1,2},{2,3},{3,4},{4,5},{5,6},{6,7},{7,8},{8,9},{9,10},{10,1... | collective-permute-start | bytes 122888 | tf_op jit(solution)/shard_map/ppermute | solution.py:161
  50.6 10.1 %collective-permute-start.15 = (f32[2,16,320]{2,1,0:T(8,128)S(1)}, f32[2,16,320]{2,1,0:T(8,128)S(1)}, u32[]{:S(2)}, u32[]{:S(2)}) collective-permute-start(f32[2,16,320]{2,1,0:T(8,128)S(1)} %get-tuple-element.85), channel_id=1, source_target_pairs={{0,31},{1,0},{2,1},{3,2},{4,3},{5,4},{6,5},{7,6},{8,7},{9,8},{10,9... | collective-permute-start | bytes 122888 | tf_op jit(solution)/shard_map/ppermute | solution.py:161
  55.4 5.4 %collective-permute-start.13 = (f32[2,16,320]{2,1,0:T(8,128)S(1)}, f32[2,16,320]{2,1,0:T(8,128)S(1)}, u32[]{:S(2)}, u32[]{:S(2)}) collective-permute-start(f32[2,16,320]{2,1,0:T(8,128)S(1)} %get-tuple-element.80.refs_6_.refs_14_), channel_id=1, source_target_pairs={{0,224},{32,0},{64,32},{96,64},{128,96},{160,128},{192,160},{224,1... | collective-permute-start | bytes 122888 | tf_op jit(solution)/shard_map/ppermute | solution.py:161
  62.4 10.1 %collective-permute-start.18 = (f32[2,16,320]{2,1,0:T(8,128)S(1)}, f32[2,16,320]{2,1,0:T(8,128)S(1)}, u32[]{:S(2)}, u32[]{:S(2)}) collective-permute-start(f32[2,16,320]{2,1,0:T(8,128)S(1)} %get-tuple-element.90), channel_id=1, source_target_pairs={{0,1},{1,2},{2,3},{3,4},{4,5},{5,6},{6,7},{7,8},{8,9},{9,10},{10,1... | collective-permute-start | bytes 122888 | tf_op jit(solution)/shard_map/ppermute | solution.py:161
  62.4 10.1 %collective-permute-start.19 = (f32[2,16,320]{2,1,0:T(8,128)S(1)}, f32[2,16,320]{2,1,0:T(8,128)S(1)}, u32[]{:S(2)}, u32[]{:S(2)}) collective-permute-start(f32[2,16,320]{2,1,0:T(8,128)S(1)} %get-tuple-element.91), channel_id=1, source_target_pairs={{0,31},{1,0},{2,1},{3,2},{4,3},{5,4},{6,5},{7,6},{8,7},{9,8},{10,9... | collective-permute-start | bytes 122888 | tf_op jit(solution)/shard_map/ppermute | solution.py:161
  67.2 5.4 %collective-permute-start.17 = (f32[2,16,320]{2,1,0:T(8,128)S(1)}, f32[2,16,320]{2,1,0:T(8,128)S(1)}, u32[]{:S(2)}, u32[]{:S(2)}) collective-permute-start(f32[2,16,320]{2,1,0:T(8,128)S(1)} %get-tuple-element.86.refs_8_.refs_16_), channel_id=1, source_target_pairs={{0,224},{32,0},{64,32},{96,64},{128,96},{160,128},{192,160},{224,1... | collective-permute-start | bytes 122888 | tf_op jit(solution)/shard_map/ppermute | solution.py:161
  74.2 10.2 %collective-permute-start.22 = (f32[2,16,320]{2,1,0:T(8,128)S(1)}, f32[2,16,320]{2,1,0:T(8,128)S(1)}, u32[]{:S(2)}, u32[]{:S(2)}) collective-permute-start(f32[2,16,320]{2,1,0:T(8,128)S(1)} %get-tuple-element.96), channel_id=1, source_target_pairs={{0,1},{1,2},{2,3},{3,4},{4,5},{5,6},{6,7},{7,8},{8,9},{9,10},{10,1... | collective-permute-start | bytes 122888 | tf_op jit(solution)/shard_map/ppermute | solution.py:161
  74.2 10.1 %collective-permute-start.23 = (f32[2,16,320]{2,1,0:T(8,128)S(1)}, f32[2,16,320]{2,1,0:T(8,128)S(1)}, u32[]{:S(2)}, u32[]{:S(2)}) collective-permute-start(f32[2,16,320]{2,1,0:T(8,128)S(1)} %get-tuple-element.97), channel_id=1, source_target_pairs={{0,31},{1,0},{2,1},{3,2},{4,3},{5,4},{6,5},{7,6},{8,7},{9,8},{10,9... | collective-permute-start | bytes 122888 | tf_op jit(solution)/shard_map/ppermute | solution.py:161
  79.0 5.4 %collective-permute-start.21 = (f32[2,16,320]{2,1,0:T(8,128)S(1)}, f32[2,16,320]{2,1,0:T(8,128)S(1)}, u32[]{:S(2)}, u32[]{:S(2)}) collective-permute-start(f32[2,16,320]{2,1,0:T(8,128)S(1)} %get-tuple-element.92.refs_10_.refs_18_), channel_id=1, source_target_pairs={{0,224},{32,0},{64,32},{96,64},{128,96},{160,128},{192,160},{224,1... | collective-permute-start | bytes 122888 | tf_op jit(solution)/shard_map/ppermute | solution.py:161
  86.0 10.2 %collective-permute-start.26 = (f32[2,16,320]{2,1,0:T(8,128)S(1)}, f32[2,16,320]{2,1,0:T(8,128)S(1)}, u32[]{:S(2)}, u32[]{:S(2)}) collective-permute-start(f32[2,16,320]{2,1,0:T(8,128)S(1)} %get-tuple-element.102), channel_id=1, source_target_pairs={{0,1},{1,2},{2,3},{3,4},{4,5},{5,6},{6,7},{7,8},{8,9},{9,10},{10,1... | collective-permute-start | bytes 122888 | tf_op jit(solution)/shard_map/ppermute | solution.py:161
  86.0 10.1 %collective-permute-start.27 = (f32[2,16,320]{2,1,0:T(8,128)S(1)}, f32[2,16,320]{2,1,0:T(8,128)S(1)}, u32[]{:S(2)}, u32[]{:S(2)}) collective-permute-start(f32[2,16,320]{2,1,0:T(8,128)S(1)} %get-tuple-element.103), channel_id=1, source_target_pairs={{0,31},{1,0},{2,1},{3,2},{4,3},{5,4},{6,5},{7,6},{8,7},{9,8},{10,9... | collective-permute-start | bytes 122888 | tf_op jit(solution)/shard_map/ppermute | solution.py:161
  90.8 5.4 %collective-permute-start.25 = (f32[2,16,320]{2,1,0:T(8,128)S(1)}, f32[2,16,320]{2,1,0:T(8,128)S(1)}, u32[]{:S(2)}, u32[]{:S(2)}) collective-permute-start(f32[2,16,320]{2,1,0:T(8,128)S(1)} %get-tuple-element.98.refs_12_.refs_20_), channel_id=1, source_target_pairs={{0,224},{32,0},{64,32},{96,64},{128,96},{160,128},{192,160},{224,1... | collective-permute-start | bytes 122888 | tf_op jit(solution)/shard_map/ppermute | solution.py:161
  97.8 10.2 %collective-permute-start.30 = (f32[2,16,320]{2,1,0:T(8,128)S(1)}, f32[2,16,320]{2,1,0:T(8,128)S(1)}, u32[]{:S(2)}, u32[]{:S(2)}) collective-permute-start(f32[2,16,320]{2,1,0:T(8,128)S(1)} %get-tuple-element.108), channel_id=1, source_target_pairs={{0,1},{1,2},{2,3},{3,4},{4,5},{5,6},{6,7},{7,8},{8,9},{9,10},{10,1... | collective-permute-start | bytes 122888 | tf_op jit(solution)/shard_map/ppermute | solution.py:161
  97.8 10.1 %collective-permute-start.31 = (f32[2,16,320]{2,1,0:T(8,128)S(1)}, f32[2,16,320]{2,1,0:T(8,128)S(1)}, u32[]{:S(2)}, u32[]{:S(2)}) collective-permute-start(f32[2,16,320]{2,1,0:T(8,128)S(1)} %get-tuple-element.109), channel_id=1, source_target_pairs={{0,31},{1,0},{2,1},{3,2},{4,3},{5,4},{6,5},{7,6},{8,7},{9,8},{10,9... | collective-permute-start | bytes 122888 | tf_op jit(solution)/shard_map/ppermute | solution.py:161
  102.6 5.4 %collective-permute-start.29 = (f32[2,16,320]{2,1,0:T(8,128)S(1)}, f32[2,16,320]{2,1,0:T(8,128)S(1)}, u32[]{:S(2)}, u32[]{:S(2)}) collective-permute-start(f32[2,16,320]{2,1,0:T(8,128)S(1)} %get-tuple-element.104.refs_14_.refs_22_), channel_id=1, source_target_pairs={{0,224},{32,0},{64,32},{96,64},{128,96},{160,128},{192,160},{224,1... | collective-permute-start | bytes 122888 | tf_op jit(solution)/shard_map/ppermute | solution.py:161
  (17 other events, 46.4 us)
